TPU v7x, 512 devices: a whole 4x8x8 slice. The times are simulated.
512 devices in a mesh: dp: 32 (over z, y_hi, core), fsdp: 16 (over y_lo, x).
Axes of the slice: x: 4, y: 8 (y_hi: 2, y_lo: 4; y = y_hi * 4 + y_lo), z: 8, core: 2. Of those that a mesh axis runs over, the one named last changes fastest.
Arguments:
- logits: bfloat16 [16384, 32000], P('dp', 'fsdp'), may hold values from -115 to 125
- labels: int32 [16384], P('dp'), may hold values from 0 to 31999
- activations: bfloat16 [16384, 5120], P('dp', 'fsdp'), may hold values from -6 to 6
- proj_in: bfloat16 [5120, 64], P('fsdp'), may hold values from -0.078125 to 0.078125
- proj_out: bfloat16 [32000, 64], P('fsdp'), may hold values from -6 to 6
Outputs:
- features: float32 [2048, 4096], P(('dp', 'fsdp'))
- gram: float32 [4096, 4096], P('fsdp', 'dp')
All inputs are finite; a program needn't handle non-finite values.
Results may differ from a plain program's by a relative error of at most 0.014.
Values may be sent and summed in bfloat16 or wider, within the bound.
A program may use at most 64 MiB of HBM per device.

v0:
```python
import jax
import jax.numpy as jnp
from jax import lax
from jax.sharding import PartitionSpec as P

SEQ = 8


def copy_for_each(value, axis):
    count = lax.axis_size(axis)
    return lax.all_to_all(
        jnp.broadcast_to(value[None], (count, *value.shape)), axis, 0, 0, tiled=True
    )


def collected_together(value, axis):
    leaves = jax.tree.leaves(value)
    sequence = sorted(range(len(leaves)), key=lambda k: -leaves[k].size)
    width = (1, *leaves[sequence[0]].shape)[-1]
    lines = [
        jnp.pad(leaves[k].reshape(-1), (0, -leaves[k].size % width)).reshape(-1, width)
        for k in sequence
    ]
    both, at, found = (copy_for_each(jnp.concatenate(lines), axis), 0, {})
    for k, line in zip(sequence, lines):
        piece = both[:, at : at + len(line)].reshape(len(both), -1)
        found[k] = piece[:, : leaves[k].size].reshape(-1, *leaves[k].shape)
        at += len(line)
    numbers = iter(range(len(leaves)))
    return jax.tree.map(lambda _: found[next(numbers)], value)


def combined_pairwise(pieces, combine):
    while len(jax.tree.leaves(pieces)[0]) > 1:
        pieces = jax.vmap(combine)(
            *(jax.tree.map(lambda part: part[side::2], pieces) for side in (0, 1))
        )
    return jax.tree.map(lambda part: part[0], pieces)


def merged(value, axis, combine):
    pieces = collected_together(value, axis)
    return combined_pairwise(pieces, combine)


def cut_along(value, dim, count):
    dims = value.shape
    tiles = value.reshape(*dims[:dim], count, dims[dim] // count, *dims[dim + 1 :])
    return jnp.moveaxis(tiles, dim, 0)


def summed_on_arrival(value, axis, dim):
    tiles = cut_along(value, dim, lax.axis_size(axis))
    arrived = lax.all_to_all(tiles, axis, split_axis=0, concat_axis=0, tiled=True)
    return arrived.sum(axis=0)


def sent_together(arrays, axis, dim, along):
    both = jnp.concatenate(arrays, axis=along)
    filled, at, done = (summed_on_arrival(both, axis, dim), 0, [])
    for a in arrays:
        done.append(lax.slice_in_dim(filled, at, at + a.shape[along], axis=along))
        at += a.shape[along]
    return tuple(done)


def joined_along(tiles, dim):
    dims = list(tiles.shape[1:])
    dims[dim] *= tiles.shape[0]
    return jnp.moveaxis(tiles, 0, dim).reshape(dims)


def collect(value, axis, dim):
    return joined_along(copy_for_each(value, axis), dim)


def combine_stats(earlier, later):
    top = jnp.maximum(earlier[0], later[0])
    total = earlier[1] * jnp.exp(earlier[0] - top) + later[1] * jnp.exp(later[0] - top)
    return (top, total)


def body(logits, labels, activations, proj_in, proj_out):
    vocab_local = logits.shape[1]
    values = logits.astype(jnp.float32)
    local_top = jnp.max(values, axis=1)
    local_total = jnp.sum(jnp.exp(values - local_top[:, None]), axis=1)
    row_top, row_sum = merged((local_top, local_total), "fsdp", combine_stats)
    prob = jnp.exp(values - row_top[:, None]) / row_sum[:, None]
    columns = lax.axis_index("fsdp") * vocab_local + lax.broadcasted_iota(
        jnp.int32, (1, vocab_local), 1
    )
    onehot = (columns == labels[:, None]).astype(jnp.float32)
    errors = (prob - onehot).astype(jnp.bfloat16)
    part_left = jnp.dot(activations, proj_in, preferred_element_type=jnp.float32)
    part_right = jnp.dot(errors, proj_out, preferred_element_type=jnp.float32)
    left, right = sent_together((part_left, part_right), "fsdp", 0, 1)
    count = left.shape[0] // SEQ
    width_in = proj_in.shape[1]
    width_out = proj_out.shape[1]
    sketch = jnp.einsum(
        "esi,esj->eij", left.reshape(count, SEQ, width_in), right.reshape(count, SEQ, width_out)
    )
    features = sketch.reshape(count, width_in * width_out)
    rounded = features.astype(jnp.bfloat16)
    feat_all = features.shape[1]
    gram_rows = feat_all // lax.axis_size("fsdp")
    row_start = lax.axis_index("fsdp") * gram_rows
    folded = collect(rounded, "fsdp", 0)
    column_share = lax.all_to_all(folded, "dp", split_axis=1, concat_axis=0, tiled=True)
    row_share = lax.dynamic_slice_in_dim(folded, row_start, gram_rows, 1)
    gram = lax.dot_general(
        collect(row_share, "dp", 0),
        column_share,
        (((0,), (0,)), ((), ())),
        preferred_element_type=jnp.float32,
    )
    return (features, gram)


def solution(mesh):
    in_specs = (P("dp", "fsdp"), P("dp"), P("dp", "fsdp"), P("fsdp", None), P("fsdp", None))
    out_specs = (P(("dp", "fsdp"), None), P("fsdp", "dp"))
    return jax.shard_map(body, mesh=mesh, in_specs=in_specs, out_specs=out_specs, check_vma=False)
```

profile of v0, /device:TPU:8, one launch (start us, length us, event | category | flops | bytes accessed | tf_op | source)
XLA Modules:
  0.0 127.7 jit_solution(853868146917032179)
XLA Ops:
  0.6 0.0 copy-start
  0.6 0.0 copy-start.1
  0.7 0.0 copy-start.3
  0.7 2.1 %reduce_max.18 = bf16[512]{0:T(512)(128)(2,1)S(1)} reduce(bf16[512,2000]{0,1:T(8,128)(2,1)} %param.5, bf16[]{:T(256)} %constant.7.clone.1), dimensions={1}, to_apply=%region_0.0 | reduce | flops 1023488 | bytes 2049026 | tf_op jit(solution)/shard_map/reduce_max | solution.py:86
  2.7 0.0 copy-start.4
  2.7 0.0 copy-start.5
  2.8 0.1 copy-done.1
  2.9 0.7 fusion.1
  3.6 0.6 broadcast_in_dim.6
  4.3 9.1 %all-to-all-start = ((f32[16,2,512]{2,1,0:T(2,128)}), f32[16,2,512]{2,1,0:T(2,128)S(1)}, u32[]{:S(2)}, u32[]{:S(2)}) async-start(f32[16,2,512]{2,1,0:T(2,128)} %broadcast_in_dim.6), calls=%async_computation | async-start | bytes 131072 | tf_op jit(solution)/shard_map/all_to_all | solution.py:11
  13.4 0.0 copy-done
  13.4 0.0 copy-done.3
  13.4 0.2 fusion.12
  13.6 6.5 %all-to-all-done = f32[16,2,512]{2,1,0:T(2,128)S(1)} async-done(((f32[16,2,512]{2,1,0:T(2,128)}), f32[16,2,512]{2,1,0:T(2,128)S(1)}, u32[]{:S(2)}, u32[]{:S(2)}) %all-to-all-start) | async-done | bytes 65568 | tf_op jit(solution)/shard_map/all_to_all | solution.py:11
  20.1 0.1 fusion.11
  20.5 0.0 copy-done.4
  20.5 0.0 copy-done.5
  20.5 1.3 fusion.6
  21.8 0.1 copy.9
  22.0 12.0 %all_to_all.36 = f32[16,32,128]{2,1,0:T(8,128)S(1)} all-to-all(f32[16,32,128]{2,1,0:T(8,128)S(1)} %bitcast.24), channel_id=1, replica_groups=mesh['dp'=32,'fsdp'=16] {'fsdp'}, dimensions={0} | all-to-all | bytes 524288 | tf_op jit(solution)/shard_map/all_to_all | solution.py:54
  34.0 0.2 fusion.9
  34.2 0.1 reshape.67
  34.4 0.0 copy-start.2
  34.4 0.2 broadcast_in_dim.7
  34.6 16.0 %all_to_all.37 = bf16[16,4,4096]{2,1,0:T(4,128)(2,1)S(1)} all-to-all(bf16[16,4,4096]{2,1,0:T(4,128)(2,1)S(1)} %broadcast_in_dim.7), channel_id=1, replica_groups=mesh['dp'=32,'fsdp'=16] {'fsdp'}, dimensions={0} | all-to-all | bytes 1048576 | tf_op jit(solution)/shard_map/all_to_all | solution.py:11
  50.6 0.5 all_to_all.28
  51.2 1.0 copy.10
  52.2 0.0 copy-done.2
  52.2 14.4 %all-to-all-start.4 = ((bf16[64,32,128]{2,0,1:T(8,128)(2,1)}), bf16[64,32,128]{2,0,1:T(8,128)(2,1)S(1)}, u32[]{:S(2)}, u32[]{:S(2)}) async-start(bf16[64,32,128]{2,0,1:T(8,128)(2,1)} %copy.10), calls=%async_computation.4 | async-start | bytes 1048576 | tf_op jit(solution)/shard_map/all_to_all | solution.py:110
  66.6 0.1 reshape.68
  66.8 22.5 %all-to-all-done.4 = bf16[64,32,128]{2,0,1:T(8,128)(2,1)S(1)} async-done(((bf16[64,32,128]{2,0,1:T(8,128)(2,1)}), bf16[64,32,128]{2,0,1:T(8,128)(2,1)S(1)}, u32[]{:S(2)}, u32[]{:S(2)}) %all-to-all-start.4) | async-done | bytes 524320 | tf_op jit(solution)/shard_map/all_to_all | solution.py:110
  89.3 0.1 broadcast_in_dim.8
  89.4 37.2 %all_to_all.38 = bf16[32,64,256]{2,1,0:T(8,128)(2,1)S(1)} all-to-all(bf16[32,64,256]{2,1,0:T(8,128)(2,1)S(1)} %broadcast_in_dim.8), channel_id=1, replica_groups=mesh['dp'=32,'fsdp'=16] {'dp'}, dimensions={0} | all-to-all | bytes 2097152 | tf_op jit(solution)/shard_map/all_to_all | solution.py:11
  126.6 1.1 convolution_bitcast_fusion
  (24 shorter events, 0.4 us)
Async XLA Ops:
  0.6 12.8 %copy-start = (bf16[512,320]{0,1:T(8,128)(2,1)S(1)}, bf16[512,320]{0,1:T(8,128)(2,1)}, u32[]{:S(2)}) copy-start(bf16[512,320]{0,1:T(8,128)(2,1)} %param.7) | copy-start | bytes 983044
  0.6 2.2 %copy-start.1 = (bf16[512,2000]{0,1:T(8,128)(2,1)S(1)}, bf16[512,2000]{0,1:T(8,128)(2,1)}, u32[]{:S(2)}) copy-start(bf16[512,2000]{0,1:T(8,128)(2,1)} %param.5) | copy-start | bytes 6144004
  0.7 12.8 %copy-start.3 = (bf16[320,64]{0,1:T(8,128)(2,1)S(1)}, bf16[320,64]{0,1:T(8,128)(2,1)}, u32[]{:S(2)}) copy-start(bf16[320,64]{0,1:T(8,128)(2,1)} %param.8) | copy-start | bytes 122884
  2.7 17.8 %copy-start.4 = (bf16[2000,64]{0,1:T(8,128)(2,1)S(1)}, bf16[2000,64]{0,1:T(8,128)(2,1)}, u32[]{:S(2)}) copy-start(bf16[2000,64]{0,1:T(8,128)(2,1)} %param.9) | copy-start | bytes 768004
  2.7 17.8 %copy-start.5 = (s32[512]{0:T(512)S(1)}, s32[512]{0:T(512)}, u32[]{:S(2)}) copy-start(s32[512]{0:T(512)} %param.6) | copy-start | bytes 6148
  4.3 15.8 %all-to-all-start = ((f32[16,2,512]{2,1,0:T(2,128)}), f32[16,2,512]{2,1,0:T(2,128)S(1)}, u32[]{:S(2)}, u32[]{:S(2)}) async-start(f32[16,2,512]{2,1,0:T(2,128)} %broadcast_in_dim.6), calls=%async_computation | async-start | bytes 131072 | tf_op jit(solution)/shard_map/all_to_all | solution.py:11
  34.4 17.8 %copy-start.2 = (f32[4,4096]{1,0:T(4,128)}, f32[4,4096]{1,0:T(4,128)S(1)}, u32[]{:S(2)}) copy-start(f32[4,4096]{1,0:T(4,128)S(1)} %reshape.67) | copy-start | bytes 196612
  52.2 37.1 %all-to-all-start.4 = ((bf16[64,32,128]{2,0,1:T(8,128)(2,1)}), bf16[64,32,128]{2,0,1:T(8,128)(2,1)S(1)}, u32[]{:S(2)}, u32[]{:S(2)}) async-start(bf16[64,32,128]{2,0,1:T(8,128)(2,1)} %copy.10), calls=%async_computation.4 | async-start | bytes 1048576 | tf_op jit(solution)/shard_map/all_to_all | solution.py:110
where the time goes:
time: 128 us
  blocking collectives  65.2 us (51%)
  waiting for transfers between devices  29 us (23%)
  starting transfers between devices  23.6 us (18%)
  local copies, waits for them, and re-layouts  3.32 us (3%)
  other arithmetic  2.95 us (2%)
  matrix products  2.82 us (2%)
    all_to_all x2, blocking collectives, copy_for_each(): lax.all_to_all(jnp.broadcast_to(value[None], (count, *value.shape)), axis...  53.2 us
    all_to_all x1, waiting for transfers between devices, body(): lax.all_to_all(folded, 'dp', split_axis=1, concat_axis=0, tiled=True)  22.5 us
    all_to_all x1, starting transfers between devices, body(): lax.all_to_all(folded, 'dp', split_axis=1, concat_axis=0, tiled=True)  14.4 us
    all_to_all x1, blocking collectives, summed_on_arrival(): lax.all_to_all(tiles, axis, split_axis=0, concat_axis=0, tiled=True)  12 us
    all_to_all x1, starting transfers between devices, copy_for_each(): lax.all_to_all(jnp.broadcast_to(value[None], (count, *value.shape)), axis...  9.13 us
    all_to_all x1, waiting for transfers between devices, copy_for_each(): lax.all_to_all(jnp.broadcast_to(value[None], (count, *value.shape)), axis...  6.46 us
  transfers between devices with their start and end apart: 2, of which 2 were waited for; matrix products, arithmetic and copies ran while one was open for 0% of the time, Pallas kernels for 0%

commit v1 on v0

v1 whole, which is shorter than its diff:
```python
import jax
import jax.numpy as jnp
from jax import lax
from jax.experimental import pallas as pl
from jax.experimental.pallas import tpu as pltpu
from jax.sharding import PartitionSpec as P

SEQ = 8
NZ, NX, NY = 8, 4, 4
GROUPS = 16
PEERS = 16
TOK = 512
TILE = 128
OWN = 32
VOC = 2000
WIDTH = 320
K = 64
EX = 4
ROWS = 64
BLK = 256
MESH = pl.DeviceIdType.MESH
F32, BF16 = jnp.float32, jnp.bfloat16


def kernel(
    logits_h, labels_h, act_h, pin_h, pout_h,
    feat_h, gram_h,
    logits, labels, act, pin, pout,
    rhs, rhs_in, labcol, left, lhs, stats,
    psend, precv, lr, feat, pieces, row_in, col_in, rows, cols, acc, xrecv, gout,
    load_sem, rs_send, rs_recv, a2a_send, a2a_recv, ag_send, row_sem, col_sem, x_send, x_recv, out_sem,
):
    d, f = lax.axis_index("dp"), lax.axis_index("fsdp")
    core, c = lax.rem(d, 2), lax.div(d, 2)
    z, yh = lax.div(c, 2), lax.rem(c, 2)
    yl, x = lax.div(f, NX), lax.rem(f, NX)

    def dev(group, peer):
        return (group * 2 + core, peer)

    loads = []
    for k, (src, dst) in enumerate(((labels_h, labels), (pout_h, pout), (pin_h, pin), (act_h, act))):
        loads.append(pltpu.make_async_copy(src, dst, load_sem.at[k]))
    quarter = [lax.rem(yl + 1 + s, NY) for s in range(NY)]
    chunks = []
    for s in range(NY):
        at = pl.ds(pl.multiple_of(quarter[s] * TILE, TILE), TILE)
        chunks.append(pltpu.make_async_copy(logits_h.at[at], logits.at[at], load_sem.at[4 + s]))
    for copy in (loads[0], loads[1], chunks[0], loads[2], loads[3], *chunks[1:]):
        copy.start()

    barrier = pltpu.get_barrier_semaphore()

    def tell(group, peer):
        pl.semaphore_signal(barrier, inc=1, device_id=dev(group, peer), device_id_type=MESH)

    z_up, z_down = lax.rem(z + 1, NZ) * 2 + yh, lax.rem(z + NZ - 1, NZ) * 2 + yh
    y_far = z * 2 + 1 - yh
    for k in range(1, PEERS):
        tell(c, lax.rem(f + k, PEERS))
    for k in range(1, PEERS):
        tell(f, lax.rem(f + k, PEERS))

    @pl.when(c != f)
    def _():
        tell(f, f)

    tell(z_up, f)
    tell(z_down, f)
    tell(y_far, f)
    other = 1 - core
    partner = (c * 2 + other, f)
    pl.semaphore_signal(barrier, inc=1, device_id=partner, device_id_type=MESH)

    lane = lax.broadcasted_iota(jnp.int32, (1, 128), 1)

    loads[0].wait()
    for q in range(NY):
        labcol[q * TILE : (q + 1) * TILE, :] = jnp.transpose(
            jnp.broadcast_to(labels[q : q + 1, :], (8, 128))
        )[:, 0:1] - f * VOC
    loads[1].wait()
    rhs[:, 0:K] = pout[...]
    rhs[:, K:128] = jnp.ones((VOC, 128 - K), BF16)

    def local_tile(s):
        q = quarter[s]
        chunks[s].wait()

        @pl.loop(0, TILE // 16)
        def _(r):
            at = pl.multiple_of(r * 16, 16)
            start = pl.multiple_of(q * TILE + at, 16)
            value = logits[pl.ds(start, 16), :].astype(F32)
            top = jnp.max(value, axis=1, keepdims=True)
            column = lax.broadcasted_iota(jnp.int32, (16, VOC), 1)
            hot = column == labcol[pl.ds(start, 16), :]
            expo = jnp.exp(value - top)
            lhs[pl.ds(at, 16), :] = jnp.where(hot, 0.0, expo).astype(BF16)
            lhs[pl.ds(TILE + at, 16), :] = jnp.where(hot, 1.0, 0.0).astype(BF16)
            at_label = jnp.sum(jnp.where(hot, value, 0.0), axis=1, keepdims=True)
            stats[pl.ds(at, 16), :] = jnp.where(lane < 112, top, at_label)

        both = jnp.dot(lhs[...], rhs[...], preferred_element_type=F32)
        a, b = both[:TILE], both[TILE:]
        low = a - a.astype(BF16).astype(F32)
        a = jnp.where(lane < 80, a, jnp.where(lane < 96, low, stats[...]))
        b = jnp.where(lane < K, b, left[pl.ds(pl.multiple_of(q * TILE, TILE), TILE), :])
        for t in range(NX):
            at = slice(t * OWN, (t + 1) * OWN)
            psend[q * NX + t, :, 0:128] = a[at].astype(BF16)
            psend[q * NX + t, :, 128:256] = b[at].astype(BF16)

    def send_share(peer):
        pltpu.make_async_remote_copy(
            src_ref=psend.at[peer], dst_ref=precv.at[f], send_sem=rs_send, recv_sem=rs_recv,
            device_id=dev(c, peer), device_id_type=MESH,
        ).start()

    for s in range(NY):
        if s == 0:
            loads[2].wait()
            loads[3].wait()
            rhs_in[:, 0:K] = jnp.zeros((WIDTH, K), BF16)
            rhs_in[:, K:128] = pin[...]
            left[...] = jnp.dot(act[...], rhs_in[...], preferred_element_type=F32)
        local_tile(s)
        if s == 0:
            @pl.when(c != f)
            def _():
                pl.semaphore_wait(barrier, 35)

            @pl.when(c == f)
            def _():
                pl.semaphore_wait(barrier, 34)

        for t in range(1, NX + 1):
            across = lax.rem(x + t, NX)
            if s < NY - 1 or t < NX:
                send_share(quarter[s] * NX + across)
    precv[f] = psend[f]

    def wait_bytes(ref, sem):
        pltpu.make_async_copy(ref, ref, sem).wait()

    wait_bytes(precv.at[pl.ds(0, PEERS - 1)], rs_recv)

    top = precv[0, :, 0:128].astype(F32)
    for k in range(1, PEERS):
        top = jnp.maximum(top, precv[k, :, 0:128].astype(F32))
    top = top[:, 96:97]
    sum_a = jnp.zeros((OWN, 128), F32)
    sum_x = jnp.zeros((OWN, 128), F32)
    sum_b = jnp.zeros((OWN, 128), F32)
    for k in range(PEERS):
        a = precv[k, :, 0:128].astype(F32)
        sum_a += jnp.exp(a[:, 96:97] - top) * a
        sum_x += a
        sum_b += precv[k, :, 128:256].astype(F32)
    rest = sum_a[:, 64:65] + sum_a[:, 80:81]
    total = rest + jnp.exp(sum_x[:, 112:113] - top)
    right = (sum_a - rest * sum_b) / total
    lr[...] = jnp.where(lane < K, right, sum_b)

    halves = []
    for s in range(SEQ // 2):
        both = jnp.concatenate(
            [lr[pl.ds(2 * s, EX, stride=SEQ), :], lr[pl.ds(2 * s + 1, EX, stride=SEQ), :]], axis=0
        )
        halves.append((both, jnp.where(lane < K, both, pltpu.roll(both, K, 1))))
    for k in range(K // 2):
        value = jnp.zeros((8, 128), F32)
        for both, wide in halves:
            first, second = both[:, K + 2 * k : K + 2 * k + 1], both[:, K + 2 * k + 1 : K + 2 * k + 2]
            value += jnp.where(lane < K, first, second) * wide
        value = value[0:EX] + value[EX:8]
        feat[:, k * 128 : (k + 1) * 128] = value
        pieces[k // 2, :, (k % 2) * 128 : (k % 2 + 1) * 128] = value.astype(BF16)
    feat_out = pltpu.make_async_copy(feat, feat_h, out_sem.at[0])
    feat_out.start()

    for k in range(1, PEERS):
        block = lax.rem(f + k, PEERS)
        pltpu.make_async_remote_copy(
            src_ref=pieces.at[block], dst_ref=row_in.at[f], send_sem=a2a_send.at[0], recv_sem=a2a_recv.at[0],
            device_id=dev(c, block), device_id_type=MESH,
        ).start()

    def send_col(block):
        pltpu.make_async_remote_copy(
            src_ref=pieces.at[block], dst_ref=col_in.at[f], send_sem=a2a_send.at[1], recv_sem=a2a_recv.at[1],
            device_id=dev(block, c), device_id_type=MESH,
        ).start()

    for k in range(1, PEERS):
        send_col(lax.rem(c + k, PEERS))

    @pl.when(c != f)
    def _():
        send_col(c)

    @pl.when(c == f)
    def _():
        col_in[f] = pieces[c]

    row_in[f] = pieces[f]
    wait_bytes(psend.at[pl.ds(0, PEERS - 1)], rs_send)

    def packed(ref):
        lines = [ref[k].astype(F32) for k in range(PEERS)]
        return jnp.concatenate(lines, axis=0).astype(BF16)

    def copy_row(chunk, target, slot):
        return pltpu.make_async_remote_copy(
            src_ref=rows.at[chunk], dst_ref=rows.at[chunk], send_sem=ag_send.at[0], recv_sem=row_sem.at[slot],
            device_id=dev(target, f), device_id_type=MESH,
        )

    def copy_col(chunk, target, slot):
        return pltpu.make_async_remote_copy(
            src_ref=cols.at[chunk], dst_ref=cols.at[chunk], send_sem=ag_send.at[1], recv_sem=col_sem.at[slot],
            device_id=dev(c, target), device_id_type=MESH,
        )

    def row_chunk(away, far):
        return lax.rem(z + NZ + away, NZ) * 2 + (1 - yh if far else yh)

    def send_row(away, far, up, slot):
        copy_row(row_chunk(away, far), z_up if up else z_down, slot).start()

    def got_row(away, far, slot):
        copy_row(row_chunk(away, far), z_up, slot).wait_recv()

    x_up, x_down = lax.rem(x + 1, NX), lax.rem(x + NX - 1, NX)
    x_two = lax.rem(x + 2, NX)

    def col_chunk(k, across):
        return lax.rem(yl + k, NY) * NX + across

    wait_bytes(row_in.at[pl.ds(0, PEERS - 1)], a2a_recv.at[0])
    rows[c] = packed(row_in)
    send_row(0, False, True, 0)
    send_row(0, False, False, 4)
    copy_row(c, y_far, 14).start()

    @pl.when(c != f)
    def _():
        wait_bytes(col_in, a2a_recv.at[1])

    @pl.when(c == f)
    def _():
        wait_bytes(col_in.at[pl.ds(0, PEERS - 1)], a2a_recv.at[1])

    cols[f] = packed(col_in)
    for k in range(1, NY):
        copy_col(f, lax.rem(yl + k, NY) * NX + x, NY - 1 - k).start()

    def col_send(k):
        copy_col(col_chunk(k, x), yl * NX + x_up, 3 + 3 * k).start()
        copy_col(col_chunk(k, x), yl * NX + x_down, 4 + 3 * k).start()

    def col_pass(k):
        copy_col(col_chunk(k, x_down), yl * NX + x_up, 3 + 3 * k).wait_recv()
        if k % 2 == 0:
            copy_col(col_chunk(k, x_down), yl * NX + x_up, 5 + 3 * k).start()
        copy_col(col_chunk(k, x_up), yl * NX + x_up, 4 + 3 * k).wait_recv()
        if k % 2 == 1:
            copy_col(col_chunk(k, x_up), yl * NX + x_down, 5 + 3 * k).start()

    col_send(0)
    wait_bytes(pieces.at[pl.ds(0, PEERS - 1)], a2a_send.at[0])

    @pl.when(c != f)
    def _():
        wait_bytes(pieces, a2a_send.at[1])

    @pl.when(c == f)
    def _():
        wait_bytes(pieces.at[pl.ds(0, PEERS - 1)], a2a_send.at[1])

    got_row(-1, False, 0)
    send_row(-1, False, True, 1)
    got_row(1, False, 4)
    send_row(1, False, False, 5)
    for k in range(1, NY):
        copy_col(col_chunk(k, x), f, k - 1).wait_recv()
        col_send(k)
    copy_row(y_far, y_far, 14).wait_recv()
    send_row(0, True, True, 7)
    send_row(0, True, False, 10)
    col_pass(0)
    got_row(-2, False, 1)
    send_row(-2, False, True, 2)
    got_row(2, False, 5)
    send_row(2, False, False, 6)
    got_row(-1, True, 7)
    send_row(-1, True, True, 8)
    got_row(1, True, 10)
    send_row(1, True, False, 11)
    for k in range(1, NY):
        col_pass(k)
    got_row(-3, False, 2)
    send_row(-3, False, True, 3)
    got_row(-2, True, 8)
    send_row(-2, True, True, 9)
    got_row(2, True, 11)
    send_row(2, True, False, 12)
    for k in range(NY):
        copy_col(col_chunk(k, x_two), f, 5 + 3 * k).wait_recv()

    def product(away):
        at = pl.ds(lax.rem(z + NZ + away, NZ) * 2, 2)
        a = rows[at].reshape(2 * ROWS, BLK)
        b = cols[at].reshape(2 * ROWS, BLK)
        return lax.dot_general(a, b, (((0,), (0,)), ((), ())), preferred_element_type=F32)

    def add(away):
        value = product(away)
        acc[0] += value[:, 0:128]
        acc[1] += value[:, 128:256]

    value = product(0)
    acc[0] = value[:, 0:128]
    acc[1] = value[:, 128:256]
    got_row(3, True, 12)
    send_row(3, True, False, 13)
    for away in (-1, 1, -2, 2):
        add(away)
    got_row(-3, True, 9)
    add(-3)
    got_row(3, False, 6)
    add(3)
    got_row(-4, False, 3)
    got_row(-4, True, 13)
    add(-4)

    swap = pltpu.make_async_remote_copy(
        src_ref=acc.at[other], dst_ref=xrecv, send_sem=x_send, recv_sem=x_recv,
        device_id=partner, device_id_type=MESH,
    )
    swap.start()
    wait_bytes(rows.at[pl.ds(0, GROUPS - 1)], ag_send.at[0])
    wait_bytes(cols.at[pl.ds(0, PEERS - 1)], ag_send.at[1])
    feat_out.wait()
    swap.wait_recv()
    gout[...] = acc[core] + xrecv[...]
    gram_out = pltpu.make_async_copy(gout, gram_h, out_sem.at[1])
    gram_out.start()
    swap.wait_send()
    gram_out.wait()


def body(logits, labels, activations, proj_in, proj_out):
    dma, vmem = pltpu.SemaphoreType.DMA, pltpu.VMEM
    return pl.pallas_call(
        kernel,
        out_shape=(
            jax.ShapeDtypeStruct((EX, K * K), F32),
            jax.ShapeDtypeStruct((BLK, BLK // 2), F32),
        ),
        in_specs=[pl.BlockSpec(memory_space=pl.ANY)] * 5,
        out_specs=(pl.BlockSpec(memory_space=pl.ANY),) * 2,
        scratch_shapes=[
            vmem((TOK, VOC), BF16),
            vmem((NY, TILE), jnp.int32),
            vmem((TOK, WIDTH), BF16),
            vmem((WIDTH, K), BF16),
            vmem((VOC, K), BF16),
            vmem((VOC, 128), BF16),
            vmem((WIDTH, 128), BF16),
            vmem((TOK, 1), jnp.int32),
            vmem((TOK, 128), F32),
            vmem((2 * TILE, VOC), BF16),
            vmem((TILE, 128), F32),
            vmem((PEERS, OWN, 256), BF16),
            vmem((PEERS, OWN, 256), BF16),
            vmem((OWN, 128), F32),
            vmem((EX, K * K), F32),
            vmem((PEERS, EX, BLK), BF16),
            vmem((PEERS, EX, BLK), BF16),
            vmem((PEERS, EX, BLK), BF16),
            vmem((GROUPS, ROWS, BLK), BF16),
            vmem((PEERS, ROWS, BLK), BF16),
            vmem((2, BLK, 128), F32),
            vmem((BLK, 128), F32),
            vmem((BLK, 128), F32),
            dma((4 + NY,)),
            dma, dma,
            dma((2,)), dma((2,)),
            dma((2,)), dma((15,)), dma((15,)),
            dma, dma,
            dma((2,)),
        ],
        compiler_params=pltpu.CompilerParams(
            collective_id=0, has_side_effects=True, vmem_limit_bytes=40 * 1024 * 1024
        ),
        cost_estimate=pl.CostEstimate(flops=500_000_000, bytes_accessed=4_000_000, transcendentals=1_100_000),
    )(logits, labels.reshape(NY, TILE), activations, proj_in, proj_out)


def solution(mesh):
    in_specs = (P("dp", "fsdp"), P("dp"), P("dp", "fsdp"), P("fsdp", None), P("fsdp", None))
    out_specs = (P(("dp", "fsdp"), None), P("fsdp", "dp"))
    return jax.shard_map(body, mesh=mesh, in_specs=in_specs, out_specs=out_specs, check_vma=False)
```

time: 128 us -> 62.2 us (0.49)
  the two profiles are of different devices: /device:TPU:8 before, /device:TPU:1 now
where the time goes in v1:
time: 62.2 us; the launch traced here: 61.9 us
  Pallas kernels  53.7 us (86%)
  local copies, waits for them, and re-layouts  7.56 us (12%)
  between operations  0.67 us (1%)
    pallas_call x1, Pallas kernels, body(): pl.pallas_call(kernel, out_shape=(jax.ShapeDtypeStruct((EX, K * K), F32),...  53.7 us
    unnamed x8, local copies, waits for them, and re-layouts  7.56 us

profile of v1, /device:TPU:1, one launch (start us, length us, event | category | flops | bytes accessed | tf_op | source)
XLA Modules:
  0.0 61.9 jit_solution(9129848039076429093)
XLA Ops:
  0.6 0.9 %copy.9.pin_h = bf16[320,64]{1,0:T(8,128)(2,1)S(1)} copy(bf16[320,64]{0,1:T(8,128)(2,1)} %param.8) | data formatting | bytes 81920 | tf_op args[3]
  1.5 1.2 %copy.8.act_h = bf16[512,320]{1,0:T(8,128)(2,1)S(1)} copy(bf16[512,320]{0,1:T(8,128)(2,1)} %param.7) | data formatting | bytes 655360 | tf_op args[2]
  2.7 1.2 %copy.10.pout_h = bf16[2000,64]{1,0:T(8,128)(2,1)S(1)} copy(bf16[2000,64]{0,1:T(8,128)(2,1)} %param.9) | data formatting | bytes 512000 | tf_op args[4]
  4.0 0.0 copy-start
  4.0 2.9 %copy.7.logits_h = bf16[512,2000]{1,0:T(8,128)(2,1)S(1)} copy(bf16[512,2000]{0,1:T(8,128)(2,1)} %param.5) | data formatting | bytes 4096000 | tf_op args[0]
  6.9 0.0 copy-done
  6.9 53.7 %shard_map.68 = (f32[4,4096]{1,0:T(4,128)S(1)}, f32[256,128]{1,0:T(8,128)S(1)}) custom-call(bf16[512,2000]{1,0:T(8,128)(2,1)S(1)} %copy.7.logits_h, s32[4,128]{1,0:T(4,128)S(1)} %bitcast.1, bf16[512,320]{1,0:T(8,128)(2,1)S(1)} %copy.8.act_h, bf16[320,64]{1,0:T(8,128)(2,1)S(1)} %copy.9.pin_h, bf16[2000,64]{1,0:T(8,128)(2,1)S(1)} %copy.10.pout_h), custom_call_target="tpu_custom_call" | custom-call | flops 500000000 | bytes 4000000 | tf_op jit(solution)/shard_map/pallas_call | solution.py:355
  60.6 0.6 %copy.13 = f32[4,4096]{1,0:T(4,128)} copy(f32[4,4096]{1,0:T(4,128)S(1)} %get-tuple-element.4) | data formatting | bytes 131072
  61.2 0.7 %copy.14 = f32[256,128]{1,0:T(8,128)} copy(f32[256,128]{1,0:T(8,128)S(1)} %get-tuple-element.5) | data formatting | bytes 262144
Async XLA Ops:
  4.0 2.9 %copy-start = (s32[512]{0:T(512)S(1)}, s32[512]{0:T(512)}, u32[]{:S(2)}) copy-start(s32[512]{0:T(512)} %param.6) | copy-start | bytes 6148

commit v2 on v1

v2 whole, which is shorter than its diff:
```python
import jax
import jax.numpy as jnp
from jax import lax
from jax.experimental import pallas as pl
from jax.experimental.pallas import tpu as pltpu
from jax.sharding import PartitionSpec as P

SEQ = 8
NZ, NX, NY = 8, 4, 4
GROUPS = 16
PEERS = 16
TOK = 512
TILE = 128
OWN = 32
VOC = 2000
WIDTH = 320
K = 64
EX = 4
ROWS = 64
BLK = 256
MESH = pl.DeviceIdType.MESH
F32, BF16 = jnp.float32, jnp.bfloat16


def kernel(
    logits_h, labels_h, act_h, pin_h, pout_h,
    feat_h, gram_h,
    logits, labels, act, pin, weights, left,
    psend, precv, lr, feat, pieces, row_in, col_in, rows, cols, acc, xrecv, gout,
    load_sem, rs_send, rs_recv, a2a_send, a2a_recv, ag_send, row_sem, col_sem, x_send, x_recv, out_sem,
):
    d, f = lax.axis_index("dp"), lax.axis_index("fsdp")
    core, c = lax.rem(d, 2), lax.div(d, 2)
    z, yh = lax.div(c, 2), lax.rem(c, 2)
    yl, x = lax.div(f, NX), lax.rem(f, NX)

    def dev(group, peer):
        return (group * 2 + core, peer)

    quarter = [lax.rem(yl + 1 + s, NY) for s in range(NY)]
    chunks = []
    for s in range(NY):
        at = pl.ds(pl.multiple_of(quarter[s] * TILE, TILE), TILE)
        chunks.append(pltpu.make_async_copy(logits_h.at[:, at], logits.at[s], load_sem.at[4 + s]))
    pairs = ((labels_h, labels), (pout_h, weights.at[0:K]), (pin_h, pin), (act_h, act))
    loads = [pltpu.make_async_copy(src, dst, load_sem.at[k]) for k, (src, dst) in enumerate(pairs)]
    for copy in (chunks[0], loads[0], loads[1], chunks[1], loads[2], loads[3], *chunks[2:]):
        copy.start()

    barrier = pltpu.get_barrier_semaphore()

    def tell(group, peer):
        pl.semaphore_signal(barrier, inc=1, device_id=dev(group, peer), device_id_type=MESH)

    def away(k):
        return lax.rem(z + NZ + k, NZ)

    y_far = z * 2 + 1 - yh
    for k in range(1, PEERS):
        tell(c, lax.rem(f + k, PEERS))
    for k in range(1, PEERS):
        tell(f, lax.rem(f + k, PEERS))

    @pl.when(c != f)
    def _():
        tell(f, f)

    for k in range(PEERS):
        tell(y_far, lax.rem(f + k, PEERS))
    for k in (-2, -1, 1, 2):
        tell(away(k) * 2 + yh, f)
    other = 1 - core
    partner = (c * 2 + other, f)
    pl.semaphore_signal(barrier, inc=1, device_id=partner, device_id_type=MESH)

    lane = lax.broadcasted_iota(jnp.int32, (1, 128), 1)

    weights[K : K + 16, :] = jnp.ones((16, VOC), BF16)

    def local_tile(s):
        q = quarter[s]
        chunks[s].wait()
        top = logits[s, 0:80, :]
        for at in range(80, VOC, 80):
            top = jnp.maximum(top, logits[s, at : at + 80, :])
        top = jnp.max(top.astype(F32), axis=0, keepdims=True)
        if s == 0:
            loads[0].wait()
            loads[1].wait()
        token = labels[pl.ds(q, 1), :] - f * VOC
        both = jnp.zeros((K + 16, 2 * TILE), F32)
        at_label = jnp.zeros((8, TILE), F32)
        for at in range(0, VOC, 256):
            size = min(256, VOC - at)
            value = logits[s, at : at + size, :].astype(F32)
            hot = lax.broadcasted_iota(jnp.int32, (size, TILE), 0) == token - at
            expo = jnp.where(hot, 0.0, jnp.exp(value - top)).astype(BF16)
            ones = jnp.where(hot, 1.0, 0.0).astype(BF16)
            at_label += jnp.sum(jnp.where(hot, value, 0.0).reshape(size // 8, 8, TILE), axis=0)
            both += jnp.dot(
                weights[:, at : at + size], jnp.concatenate([expo, ones], axis=1), preferred_element_type=F32
            )
        at_label = jnp.sum(at_label, axis=0, keepdims=True)
        total = both[K : K + 16, :TILE]
        low = total - total.astype(BF16).astype(F32)
        wide = (16, TILE)
        a = jnp.concatenate(
            [both[:K, :TILE], total, low, jnp.broadcast_to(top, wide), jnp.broadcast_to(at_label, wide)], axis=0
        )
        b = jnp.concatenate([both[:K, TILE:], left[q]], axis=0)
        a, b = a.T, b.T
        for t in range(NX):
            at = slice(t * OWN, (t + 1) * OWN)
            psend[q * NX + t, :, 0:128] = a[at].astype(BF16)
            psend[q * NX + t, :, 128:256] = b[at].astype(BF16)

    def send_share(peer):
        pltpu.make_async_remote_copy(
            src_ref=psend.at[peer], dst_ref=precv.at[f], send_sem=rs_send, recv_sem=rs_recv,
            device_id=dev(c, peer), device_id_type=MESH,
        ).start()

    for s in range(NY):
        if s == 0:
            loads[2].wait()
            loads[3].wait()
            both = jnp.dot(pin[...], act[...], preferred_element_type=F32)
            for q in range(NY):
                left[q] = both[:, q * TILE : (q + 1) * TILE]
        local_tile(s)
        if s == 0:
            @pl.when(c != f)
            def _():
                pl.semaphore_wait(barrier, 52)

            @pl.when(c == f)
            def _():
                pl.semaphore_wait(barrier, 51)

        for t in range(1, NX + 1):
            across = lax.rem(x + t, NX)
            if s < NY - 1 or t < NX:
                send_share(quarter[s] * NX + across)
    precv[f] = psend[f]

    def wait_bytes(ref, sem):
        pltpu.make_async_copy(ref, ref, sem).wait()

    wait_bytes(precv.at[pl.ds(0, PEERS - 1)], rs_recv)

    top = precv[0, :, 0:128].astype(F32)
    for k in range(1, PEERS):
        top = jnp.maximum(top, precv[k, :, 0:128].astype(F32))
    top = top[:, 96:97]
    sum_a = jnp.zeros((OWN, 128), F32)
    sum_x = jnp.zeros((OWN, 128), F32)
    sum_b = jnp.zeros((OWN, 128), F32)
    for k in range(PEERS):
        a = precv[k, :, 0:128].astype(F32)
        sum_a += jnp.exp(a[:, 96:97] - top) * a
        sum_x += a
        sum_b += precv[k, :, 128:256].astype(F32)
    rest = sum_a[:, 64:65] + sum_a[:, 80:81]
    total = rest + jnp.exp(sum_x[:, 112:113] - top)
    right = (sum_a - rest * sum_b) / total
    lr[...] = jnp.where(lane < K, right, sum_b)

    halves = []
    for s in range(SEQ // 2):
        both = jnp.concatenate(
            [lr[pl.ds(2 * s, EX, stride=SEQ), :], lr[pl.ds(2 * s + 1, EX, stride=SEQ), :]], axis=0
        )
        halves.append((both, jnp.where(lane < K, both, pltpu.roll(both, K, 1))))
    for k in range(K // 2):
        value = jnp.zeros((8, 128), F32)
        for both, wide in halves:
            first, second = both[:, K + 2 * k : K + 2 * k + 1], both[:, K + 2 * k + 1 : K + 2 * k + 2]
            value += jnp.where(lane < K, first, second) * wide
        value = value[0:EX] + value[EX:8]
        feat[:, k * 128 : (k + 1) * 128] = value
        pieces[k // 2, :, (k % 2) * 128 : (k % 2 + 1) * 128] = value.astype(BF16)
    feat_out = pltpu.make_async_copy(feat, feat_h, out_sem.at[0])
    feat_out.start()

    def send_row(group, block):
        pltpu.make_async_remote_copy(
            src_ref=pieces.at[block], dst_ref=row_in.at[yh * PEERS + f], send_sem=a2a_send.at[0],
            recv_sem=a2a_recv.at[0], device_id=dev(group, block), device_id_type=MESH,
        ).start()

    for k in range(1, PEERS):
        send_row(y_far, lax.rem(f + k, PEERS))
        send_row(c, lax.rem(f + k, PEERS))
    send_row(y_far, f)

    def send_col(block):
        pltpu.make_async_remote_copy(
            src_ref=pieces.at[block], dst_ref=col_in.at[f], send_sem=a2a_send.at[1], recv_sem=a2a_recv.at[1],
            device_id=dev(block, c), device_id_type=MESH,
        ).start()

    for k in range(1, PEERS):
        send_col(lax.rem(c + k, PEERS))

    @pl.when(c != f)
    def _():
        send_col(c)

    @pl.when(c == f)
    def _():
        col_in[f] = pieces[c]

    row_in[yh * PEERS + f] = pieces[f]
    wait_bytes(psend.at[pl.ds(0, PEERS - 1)], rs_send)

    def packed(ref, first):
        lines = [ref[first + k].astype(F32) for k in range(PEERS)]
        return jnp.concatenate(lines, axis=0).astype(BF16)

    def copy_row(origin, half, target, up, hops):
        at = pl.ds(half * ROWS, ROWS)
        ref = rows.at[away(origin), at]
        return pltpu.make_async_remote_copy(
            src_ref=ref, dst_ref=ref, send_sem=ag_send.at[0], recv_sem=row_sem.at[(half * 2 + up) * 4 + hops - 1],
            device_id=dev(away(target) * 2 + yh, f), device_id_type=MESH,
        )

    def copy_col(chunk, target, slot):
        return pltpu.make_async_remote_copy(
            src_ref=cols.at[chunk], dst_ref=cols.at[chunk], send_sem=ag_send.at[1], recv_sem=col_sem.at[slot],
            device_id=dev(c, target), device_id_type=MESH,
        )

    x_up, x_down = lax.rem(x + 1, NX), lax.rem(x + NX - 1, NX)
    x_two = lax.rem(x + 2, NX)

    def col_chunk(k, across):
        return lax.rem(yl + k, NY) * NX + across

    wait_bytes(row_in.at[pl.ds(0, 2 * PEERS - 1)], a2a_recv.at[0])
    for half in range(2):
        rows[z, half * ROWS : (half + 1) * ROWS, :] = packed(row_in, half * PEERS)
    for hops in (2, 1):
        for half in range(2):
            copy_row(0, half, hops, 1, hops).start()
            copy_row(0, half, -hops, 0, hops).start()

    @pl.when(c != f)
    def _():
        wait_bytes(col_in, a2a_recv.at[1])

    @pl.when(c == f)
    def _():
        wait_bytes(col_in.at[pl.ds(0, PEERS - 1)], a2a_recv.at[1])

    cols[f] = packed(col_in, 0)
    for k in range(1, NY):
        copy_col(f, lax.rem(yl + k, NY) * NX + x, NY - 1 - k).start()

    def col_send(k):
        copy_col(col_chunk(k, x), yl * NX + x_up, 3 + 3 * k).start()
        copy_col(col_chunk(k, x), yl * NX + x_down, 4 + 3 * k).start()

    def col_pass(k):
        copy_col(col_chunk(k, x_down), yl * NX + x_up, 3 + 3 * k).wait_recv()
        if k % 2 == 0:
            copy_col(col_chunk(k, x_down), yl * NX + x_up, 5 + 3 * k).start()
        copy_col(col_chunk(k, x_up), yl * NX + x_up, 4 + 3 * k).wait_recv()
        if k % 2 == 1:
            copy_col(col_chunk(k, x_up), yl * NX + x_down, 5 + 3 * k).start()

    col_send(0)
    wait_bytes(row_in.at[pl.ds(0, 2 * PEERS - 1)], a2a_send.at[0])

    @pl.when(c != f)
    def _():
        wait_bytes(pieces, a2a_send.at[1])

    @pl.when(c == f)
    def _():
        wait_bytes(pieces.at[pl.ds(0, PEERS - 1)], a2a_send.at[1])

    for half in range(2):
        for up, sign in ((1, 1), (0, -1)):
            copy_row(-2 * sign, half, 1, up, 2).wait_recv()
            if up != half:
                copy_row(-2 * sign, half, 2 * sign, up, 4).start()
            copy_row(-2 * sign, half, sign, up, 3).start()
    for k in range(1, NY):
        copy_col(col_chunk(k, x), f, k - 1).wait_recv()
        col_send(k)
    for k in range(NY):
        col_pass(k)
    for k in range(NY):
        copy_col(col_chunk(k, x_two), f, 5 + 3 * k).wait_recv()

    def product(k):
        at = away(k)
        b = cols[pl.ds(at * 2, 2)].reshape(2 * ROWS, BLK)
        return lax.dot_general(rows[at], b, (((0,), (0,)), ((), ())), preferred_element_type=F32)

    total = product(0)
    for hops in (2, 1, 3):
        for up, sign in ((1, 1), (0, -1)):
            for half in range(2):
                if hops != 2:
                    copy_row(-hops * sign, half, 1, up, hops).wait_recv()
            total += product(-hops * sign)
    copy_row(-4, 0, 1, 1, 4).wait_recv()
    copy_row(-4, 1, 1, 0, 4).wait_recv()
    total += product(-4)
    acc[0] = total[:, 0:128]
    acc[1] = total[:, 128:256]

    swap = pltpu.make_async_remote_copy(
        src_ref=acc.at[other], dst_ref=xrecv, send_sem=x_send, recv_sem=x_recv,
        device_id=partner, device_id_type=MESH,
    )
    swap.start()
    wait_bytes(rows.at[pl.ds(0, NZ - 1)], ag_send.at[0])
    wait_bytes(cols.at[pl.ds(0, PEERS - 1)], ag_send.at[1])
    feat_out.wait()
    swap.wait_recv()
    gout[...] = acc[core] + xrecv[...]
    gram_out = pltpu.make_async_copy(gout, gram_h, out_sem.at[1])
    gram_out.start()
    swap.wait_send()
    gram_out.wait()


def body(logits, labels, activations, proj_in, proj_out):
    dma, vmem = pltpu.SemaphoreType.DMA, pltpu.VMEM
    return pl.pallas_call(
        kernel,
        out_shape=(
            jax.ShapeDtypeStruct((EX, K * K), F32),
            jax.ShapeDtypeStruct((BLK, BLK // 2), F32),
        ),
        in_specs=[pl.BlockSpec(memory_space=pltpu.HBM)] * 5,
        out_specs=(pl.BlockSpec(memory_space=pltpu.HBM),) * 2,
        scratch_shapes=[
            vmem((NY, VOC, TILE), BF16),
            vmem((NY, TILE), jnp.int32),
            vmem((WIDTH, TOK), BF16),
            vmem((K, WIDTH), BF16),
            vmem((K + 16, VOC), BF16),
            vmem((NY, K, TILE), F32),
            vmem((PEERS, OWN, 256), BF16),
            vmem((PEERS, OWN, 256), BF16),
            vmem((OWN, 128), F32),
            vmem((EX, K * K), F32),
            vmem((PEERS, EX, BLK), BF16),
            vmem((2 * PEERS, EX, BLK), BF16),
            vmem((PEERS, EX, BLK), BF16),
            vmem((NZ, 2 * ROWS, BLK), BF16),
            vmem((PEERS, ROWS, BLK), BF16),
            vmem((2, BLK, 128), F32),
            vmem((BLK, 128), F32),
            vmem((BLK, 128), F32),
            dma((4 + NY,)),
            dma, dma,
            dma((2,)), dma((2,)),
            dma((2,)), dma((16,)), dma((15,)),
            dma, dma,
            dma((2,)),
        ],
        compiler_params=pltpu.CompilerParams(
            collective_id=0, has_side_effects=True, vmem_limit_bytes=58 * 1024 * 1024
        ),
        cost_estimate=pl.CostEstimate(flops=500_000_000, bytes_accessed=4_000_000, transcendentals=1_100_000),
    )(logits.T, labels.reshape(NY, TILE), activations.T, proj_in.T, proj_out.T)


def solution(mesh):
    in_specs = (P("dp", "fsdp"), P("dp"), P("dp", "fsdp"), P("fsdp", None), P("fsdp", None))
    out_specs = (P(("dp", "fsdp"), None), P("fsdp", "dp"))
    return jax.shard_map(body, mesh=mesh, in_specs=in_specs, out_specs=out_specs, check_vma=False)
```

time: 62.2 us -> 51.7 us (0.83)
  Pallas kernels: 53.7 us -> 47.8 us
  local copies, waits for them, and re-layouts: 7.56 us -> 3.04 us
    pallas_call x1, Pallas kernels: 53.7 us -> 47.8 us  [body(): pl.pallas_call(kernel, out_shape=(jax.ShapeDtypeStruct((EX, K * K), F32),...]
    unnamed x8 -> x2, local copies, waits for them, and re-layouts: 7.56 us -> 3.04 us
where the time goes in v2:
time: 51.7 us; the launch traced here: 51.5 us
  Pallas kernels  47.8 us (92%)
  local copies, waits for them, and re-layouts  3.04 us (6%)
  between operations  0.64 us (1%)
    pallas_call x1, Pallas kernels, body(): pl.pallas_call(kernel, out_shape=(jax.ShapeDtypeStruct((EX, K * K), F32),...  47.8 us
    unnamed x2, local copies, waits for them, and re-layouts  3.04 us

profile of v2, /device:TPU:1, one launch (start us, length us, event | category | flops | bytes accessed | tf_op | source)
XLA Modules:
  0.0 51.5 jit_solution(102510562936675196)
XLA Ops:
  0.6 47.8 %shard_map.68 = (f32[4,4096]{1,0:T(4,128)}, f32[256,128]{1,0:T(8,128)}) custom-call(bf16[2000,512]{1,0:T(8,128)(2,1)} %bitcast.5, s32[4,128]{1,0:T(4,128)} %bitcast.9, bf16[320,512]{1,0:T(8,128)(2,1)} %bitcast.6, bf16[64,320]{1,0:T(8,128)(2,1)} %bitcast.8, bf16[64,2000]{1,0:T(8,128)(2,1)} %bitcast.7), custom_call_target="tpu_custom_call" | custom-call | flops 500000000 | bytes 4000000 | tf_op jit(solution)/shard_map/pallas_call | solution.py:333
  48.4 1.5 %copy.9 = f32[4,4096]{1,0:T(4,128)} copy(f32[4,4096]{1,0:T(4,128)} %get-tuple-element.4) | data formatting | bytes 131072
  49.9 1.6 %copy.10 = f32[256,128]{1,0:T(8,128)} copy(f32[256,128]{1,0:T(8,128)} %get-tuple-element.5) | data formatting | bytes 262144

commit v3 on v2

--- a/solution.py
+++ b/solution.py
@@ -58,15 +58,12 @@
     y_far = z * 2 + 1 - yh
     for k in range(1, PEERS):
         tell(c, lax.rem(f + k, PEERS))
-    for k in range(1, PEERS):
-        tell(f, lax.rem(f + k, PEERS))
 
     @pl.when(c != f)
     def _():
-        tell(f, f)
-
-    for k in range(PEERS):
-        tell(y_far, lax.rem(f + k, PEERS))
+        tell(f, c)
+
+    tell(y_far, f)
     for k in (-2, -1, 1, 2):
         tell(away(k) * 2 + yh, f)
     other = 1 - core
@@ -131,11 +128,11 @@
         if s == 0:
             @pl.when(c != f)
             def _():
-                pl.semaphore_wait(barrier, 52)
+                pl.semaphore_wait(barrier, 22)
 
             @pl.when(c == f)
             def _():
-                pl.semaphore_wait(barrier, 51)
+                pl.semaphore_wait(barrier, 21)
 
         for t in range(1, NX + 1):
             across = lax.rem(x + t, NX)
@@ -182,16 +179,16 @@
     feat_out = pltpu.make_async_copy(feat, feat_h, out_sem.at[0])
     feat_out.start()
 
-    def send_row(group, block):
+    def send_row(group, block, far):
         pltpu.make_async_remote_copy(
-            src_ref=pieces.at[block], dst_ref=row_in.at[yh * PEERS + f], send_sem=a2a_send.at[0],
-            recv_sem=a2a_recv.at[0], device_id=dev(group, block), device_id_type=MESH,
+            src_ref=pieces.at[block], dst_ref=row_in.at[far, f], send_sem=a2a_send.at[2 * far],
+            recv_sem=a2a_recv.at[2 * far], device_id=dev(group, block), device_id_type=MESH,
         ).start()
 
     for k in range(1, PEERS):
-        send_row(y_far, lax.rem(f + k, PEERS))
-        send_row(c, lax.rem(f + k, PEERS))
-    send_row(y_far, f)
+        send_row(c, lax.rem(f + k, PEERS), 0)
+    for k in range(PEERS):
+        send_row(y_far, lax.rem(f + k, PEERS), 1)
 
     def send_col(block):
         pltpu.make_async_remote_copy(
@@ -210,20 +207,33 @@
     def _():
         col_in[f] = pieces[c]
 
-    row_in[yh * PEERS + f] = pieces[f]
+    row_in[0, f] = pieces[f]
     wait_bytes(psend.at[pl.ds(0, PEERS - 1)], rs_send)
 
-    def packed(ref, first):
-        lines = [ref[first + k].astype(F32) for k in range(PEERS)]
+    def packed(ref):
+        lines = [ref[k].astype(F32) for k in range(PEERS)]
         return jnp.concatenate(lines, axis=0).astype(BF16)
 
-    def copy_row(origin, half, target, up, hops):
-        at = pl.ds(half * ROWS, ROWS)
-        ref = rows.at[away(origin), at]
+    sides = [pl.ds(pl.multiple_of(half * ROWS, ROWS), ROWS) for half in (yh, 1 - yh)]
+
+    def copy_row(origin, far, target, up, hops):
+        ref = rows.at[away(origin), sides[far]]
         return pltpu.make_async_remote_copy(
-            src_ref=ref, dst_ref=ref, send_sem=ag_send.at[0], recv_sem=row_sem.at[(half * 2 + up) * 4 + hops - 1],
+            src_ref=ref, dst_ref=ref, send_sem=ag_send.at[0], recv_sem=row_sem.at[(far * 2 + up) * 4 + hops - 1],
             device_id=dev(away(target) * 2 + yh, f), device_id_type=MESH,
         )
+
+    def row_start(far):
+        rows[z, sides[far], :] = packed(row_in.at[far])
+        copy_row(0, far, 2, 1, 2).start()
+        copy_row(0, far, -2, 0, 2).start()
+
+    def row_pass(far):
+        for up, sign in ((1, 1), (0, -1)):
+            copy_row(-2 * sign, far, 1, up, 2).wait_recv()
+            if up != far:
+                copy_row(-2 * sign, far, 2 * sign, up, 4).start()
+            copy_row(-2 * sign, far, sign, up, 3).start()
 
     def copy_col(chunk, target, slot):
         return pltpu.make_async_remote_copy(
@@ -237,13 +247,10 @@
     def col_chunk(k, across):
         return lax.rem(yl + k, NY) * NX + across
 
-    wait_bytes(row_in.at[pl.ds(0, 2 * PEERS - 1)], a2a_recv.at[0])
-    for half in range(2):
-        rows[z, half * ROWS : (half + 1) * ROWS, :] = packed(row_in, half * PEERS)
-    for hops in (2, 1):
-        for half in range(2):
-            copy_row(0, half, hops, 1, hops).start()
-            copy_row(0, half, -hops, 0, hops).start()
+    wait_bytes(row_in.at[0, pl.ds(0, PEERS - 1)], a2a_recv.at[0])
+    row_start(0)
+    wait_bytes(row_in.at[1], a2a_recv.at[2])
+    row_start(1)
 
     @pl.when(c != f)
     def _():
@@ -253,7 +260,7 @@
     def _():
         wait_bytes(col_in.at[pl.ds(0, PEERS - 1)], a2a_recv.at[1])
 
-    cols[f] = packed(col_in, 0)
+    cols[f] = packed(col_in)
     for k in range(1, NY):
         copy_col(f, lax.rem(yl + k, NY) * NX + x, NY - 1 - k).start()
 
@@ -270,7 +277,8 @@
             copy_col(col_chunk(k, x_up), yl * NX + x_down, 5 + 3 * k).start()
 
     col_send(0)
-    wait_bytes(row_in.at[pl.ds(0, 2 * PEERS - 1)], a2a_send.at[0])
+    wait_bytes(row_in.at[0, pl.ds(0, PEERS - 1)], a2a_send.at[0])
+    wait_bytes(row_in.at[1], a2a_send.at[2])
 
     @pl.when(c != f)
     def _():
@@ -280,35 +288,34 @@
     def _():
         wait_bytes(pieces.at[pl.ds(0, PEERS - 1)], a2a_send.at[1])
 
-    for half in range(2):
-        for up, sign in ((1, 1), (0, -1)):
-            copy_row(-2 * sign, half, 1, up, 2).wait_recv()
-            if up != half:
-                copy_row(-2 * sign, half, 2 * sign, up, 4).start()
-            copy_row(-2 * sign, half, sign, up, 3).start()
-    for k in range(1, NY):
+    for far in (0, 1):
+        copy_row(0, far, 1, 1, 1).start()
+        copy_row(0, far, -1, 0, 1).start()
+    row_pass(0)
+    for k in (1, 3, 2):
         copy_col(col_chunk(k, x), f, k - 1).wait_recv()
         col_send(k)
-    for k in range(NY):
+    col_pass(0)
+    row_pass(1)
+    for k in (1, 3, 2):
         col_pass(k)
-    for k in range(NY):
-        copy_col(col_chunk(k, x_two), f, 5 + 3 * k).wait_recv()
-
-    def product(k):
-        at = away(k)
+    for hops in (1, 3):
+        for far in (0, 1):
+            for up, sign in ((1, 1), (0, -1)):
+                copy_row(-hops * sign, far, 1, up, hops).wait_recv()
+    copy_row(-4, 0, 1, 1, 4).wait_recv()
+    copy_row(-4, 1, 1, 0, 4).wait_recv()
+
+    def product(at):
         b = cols[pl.ds(at * 2, 2)].reshape(2 * ROWS, BLK)
         return lax.dot_general(rows[at], b, (((0,), (0,)), ((), ())), preferred_element_type=F32)
 
-    total = product(0)
-    for hops in (2, 1, 3):
-        for up, sign in ((1, 1), (0, -1)):
-            for half in range(2):
-                if hops != 2:
-                    copy_row(-hops * sign, half, 1, up, hops).wait_recv()
-            total += product(-hops * sign)
-    copy_row(-4, 0, 1, 1, 4).wait_recv()
-    copy_row(-4, 1, 1, 0, 4).wait_recv()
-    total += product(-4)
+    total = jnp.zeros((BLK, BLK), F32)
+    for k in (0, 1, 3, 2):
+        total += product(lax.rem(yl + k, NY) * 2 + lax.div(x, 2))
+    for k in (0, 1, 3, 2):
+        copy_col(col_chunk(k, x_two), f, 5 + 3 * k).wait_recv()
+        total += product(lax.rem(yl + k, NY) * 2 + 1 - lax.div(x, 2))
     acc[0] = total[:, 0:128]
     acc[1] = total[:, 128:256]
 
@@ -350,7 +357,7 @@
             vmem((OWN, 128), F32),
             vmem((EX, K * K), F32),
             vmem((PEERS, EX, BLK), BF16),
-            vmem((2 * PEERS, EX, BLK), BF16),
+            vmem((2, PEERS, EX, BLK), BF16),
             vmem((PEERS, EX, BLK), BF16),
             vmem((NZ, 2 * ROWS, BLK), BF16),
             vmem((PEERS, ROWS, BLK), BF16),
@@ -359,7 +366,7 @@
             vmem((BLK, 128), F32),
             dma((4 + NY,)),
             dma, dma,
-            dma((2,)), dma((2,)),
+            dma((3,)), dma((3,)),
             dma((2,)), dma((16,)), dma((15,)),
             dma, dma,
             dma((2,)),

time: 51.7 us -> 49.9 us (0.965)
  Pallas kernels: 47.8 us -> 46 us
    pallas_call x1, Pallas kernels: 47.8 us -> 46 us  [body(): pl.pallas_call(kernel, out_shape=(jax.ShapeDtypeStruct((EX, K * K), F32),...]
where the time goes in v3:
time: 49.9 us; the launch traced here: 49.7 us
  Pallas kernels  46 us (92%)
  local copies, waits for them, and re-layouts  3.04 us (6%)
  between operations  0.64 us (1%)
    pallas_call x1, Pallas kernels, body(): pl.pallas_call(kernel, out_shape=(jax.ShapeDtypeStruct((EX, K * K), F32),...  46 us
    unnamed x2, local copies, waits for them, and re-layouts  3.04 us

profile of v3, /device:TPU:1, one launch (start us, length us, event | category | flops | bytes accessed | tf_op | source)
XLA Modules:
  0.0 49.7 jit_solution(5024467819951716427)
XLA Ops:
  0.6 46.0 %shard_map.68 = (f32[4,4096]{1,0:T(4,128)}, f32[256,128]{1,0:T(8,128)}) custom-call(bf16[2000,512]{1,0:T(8,128)(2,1)} %bitcast.5, s32[4,128]{1,0:T(4,128)} %bitcast.9, bf16[320,512]{1,0:T(8,128)(2,1)} %bitcast.6, bf16[64,320]{1,0:T(8,128)(2,1)} %bitcast.8, bf16[64,2000]{1,0:T(8,128)(2,1)} %bitcast.7), custom_call_target="tpu_custom_call" | custom-call | flops 500000000 | bytes 4000000 | tf_op jit(solution)/shard_map/pallas_call | solution.py:340
  46.7 1.5 %copy.9 = f32[4,4096]{1,0:T(4,128)} copy(f32[4,4096]{1,0:T(4,128)} %get-tuple-element.4) | data formatting | bytes 131072
  48.2 1.6 %copy.10 = f32[256,128]{1,0:T(8,128)} copy(f32[256,128]{1,0:T(8,128)} %get-tuple-element.5) | data formatting | bytes 262144

commit v4 on v3

--- a/solution.py
+++ b/solution.py
@@ -24,10 +24,10 @@
 
 def kernel(
     logits_h, labels_h, act_h, pin_h, pout_h,
-    feat_h, gram_h,
+    feat, gout,
     logits, labels, act, pin, weights, left,
-    psend, precv, lr, feat, pieces, row_in, col_in, rows, cols, acc, xrecv, gout,
-    load_sem, rs_send, rs_recv, a2a_send, a2a_recv, ag_send, row_sem, col_sem, x_send, x_recv, out_sem,
+    psend, psum, xin, yin, lr, pieces, row_in, col_in, rows, cols, acc, xrecv,
+    load_sem, rs_send, xin_sem, yin_sem, a2a_send, a2a_recv, ag_send, row_sem, col_sem, x_send, x_recv,
 ):
     d, f = lax.axis_index("dp"), lax.axis_index("fsdp")
     core, c = lax.rem(d, 2), lax.div(d, 2)
@@ -56,8 +56,10 @@
         return lax.rem(z + NZ + k, NZ)
 
     y_far = z * 2 + 1 - yh
-    for k in range(1, PEERS):
-        tell(c, lax.rem(f + k, PEERS))
+    for k in range(1, NX):
+        tell(c, yl * NX + lax.rem(x + k, NX))
+    for k in range(1, NY):
+        tell(c, lax.rem(yl + k, NY) * NX + x)
 
     @pl.when(c != f)
     def _():
@@ -111,11 +113,43 @@
             psend[q * NX + t, :, 0:128] = a[at].astype(BF16)
             psend[q * NX + t, :, 128:256] = b[at].astype(BF16)
 
-    def send_share(peer):
+    def send_x(s, across):
         pltpu.make_async_remote_copy(
-            src_ref=psend.at[peer], dst_ref=precv.at[f], send_sem=rs_send, recv_sem=rs_recv,
-            device_id=dev(c, peer), device_id_type=MESH,
+            src_ref=psend.at[quarter[s] * NX + across], dst_ref=xin.at[s, x], send_sem=rs_send,
+            recv_sem=xin_sem.at[s], device_id=dev(c, yl * NX + across), device_id_type=MESH,
         ).start()
+
+    def merged(parts):
+        parts = [(part[:, 0:128].astype(F32), part[:, 128:256].astype(F32)) for part in parts]
+        top = parts[0][0]
+        for a, _ in parts[1:]:
+            top = jnp.maximum(top, a)
+        top = top[:, 96:97]
+        sum_a, sum_x, sum_b = (jnp.zeros((OWN, 128), F32) for _ in range(3))
+        for a, b in parts:
+            sum_a += jnp.exp(a[:, 96:97] - top) * a
+            sum_x += a
+            sum_b += b
+        return top, sum_a, sum_x, sum_b, sum_a[:, 64:65] + sum_a[:, 80:81]
+
+    def merge_x(s):
+        xin[s, x] = psend[quarter[s] * NX + x]
+        wait_bytes(xin.at[s, pl.ds(0, NX - 1)], xin_sem.at[s])
+        top, sum_a, sum_x, sum_b, rest = merged([xin[s, k] for k in range(NX)])
+        low = rest - rest.astype(BF16).astype(F32)
+        a = jnp.where(lane < 80, jnp.where(lane < K, sum_a, rest), jnp.where(lane < 96, low, top))
+        a = jnp.where(lane < 112, a, sum_x)
+        return jnp.concatenate([a, sum_b], axis=1).astype(BF16)
+
+    def send_y(s):
+        psum[s] = merge_x(s)
+        pltpu.make_async_remote_copy(
+            src_ref=psum.at[s], dst_ref=yin.at[yl], send_sem=rs_send, recv_sem=yin_sem,
+            device_id=dev(c, quarter[s] * NX + x), device_id_type=MESH,
+        ).start()
+
+    def wait_bytes(ref, sem):
+        pltpu.make_async_copy(ref, ref, sem).wait()
 
     for s in range(NY):
         if s == 0:
@@ -128,36 +162,19 @@
         if s == 0:
             @pl.when(c != f)
             def _():
-                pl.semaphore_wait(barrier, 22)
+                pl.semaphore_wait(barrier, 13)
 
             @pl.when(c == f)
             def _():
-                pl.semaphore_wait(barrier, 21)
-
-        for t in range(1, NX + 1):
-            across = lax.rem(x + t, NX)
-            if s < NY - 1 or t < NX:
-                send_share(quarter[s] * NX + across)
-    precv[f] = psend[f]
-
-    def wait_bytes(ref, sem):
-        pltpu.make_async_copy(ref, ref, sem).wait()
-
-    wait_bytes(precv.at[pl.ds(0, PEERS - 1)], rs_recv)
-
-    top = precv[0, :, 0:128].astype(F32)
-    for k in range(1, PEERS):
-        top = jnp.maximum(top, precv[k, :, 0:128].astype(F32))
-    top = top[:, 96:97]
-    sum_a = jnp.zeros((OWN, 128), F32)
-    sum_x = jnp.zeros((OWN, 128), F32)
-    sum_b = jnp.zeros((OWN, 128), F32)
-    for k in range(PEERS):
-        a = precv[k, :, 0:128].astype(F32)
-        sum_a += jnp.exp(a[:, 96:97] - top) * a
-        sum_x += a
-        sum_b += precv[k, :, 128:256].astype(F32)
-    rest = sum_a[:, 64:65] + sum_a[:, 80:81]
+                pl.semaphore_wait(barrier, 12)
+
+        for t in range(1, NX):
+            send_x(s, lax.rem(x + t, NX))
+    for s in range(NY - 1):
+        send_y(s)
+    yin[yl] = merge_x(NY - 1)
+    wait_bytes(yin.at[pl.ds(0, NY - 1)], yin_sem)
+    top, sum_a, sum_x, sum_b, rest = merged([yin[k] for k in range(NY)])
     total = rest + jnp.exp(sum_x[:, 112:113] - top)
     right = (sum_a - rest * sum_b) / total
     lr[...] = jnp.where(lane < K, right, sum_b)
@@ -176,8 +193,6 @@
         value = value[0:EX] + value[EX:8]
         feat[:, k * 128 : (k + 1) * 128] = value
         pieces[k // 2, :, (k % 2) * 128 : (k % 2 + 1) * 128] = value.astype(BF16)
-    feat_out = pltpu.make_async_copy(feat, feat_h, out_sem.at[0])
-    feat_out.start()
 
     def send_row(group, block, far):
         pltpu.make_async_remote_copy(
@@ -326,13 +341,9 @@
     swap.start()
     wait_bytes(rows.at[pl.ds(0, NZ - 1)], ag_send.at[0])
     wait_bytes(cols.at[pl.ds(0, PEERS - 1)], ag_send.at[1])
-    feat_out.wait()
     swap.wait_recv()
     gout[...] = acc[core] + xrecv[...]
-    gram_out = pltpu.make_async_copy(gout, gram_h, out_sem.at[1])
-    gram_out.start()
     swap.wait_send()
-    gram_out.wait()
 
 
 def body(logits, labels, activations, proj_in, proj_out):
@@ -344,7 +355,7 @@
             jax.ShapeDtypeStruct((BLK, BLK // 2), F32),
         ),
         in_specs=[pl.BlockSpec(memory_space=pltpu.HBM)] * 5,
-        out_specs=(pl.BlockSpec(memory_space=pltpu.HBM),) * 2,
+        out_specs=(pl.BlockSpec(memory_space=pltpu.VMEM),) * 2,
         scratch_shapes=[
             vmem((NY, VOC, TILE), BF16),
             vmem((NY, TILE), jnp.int32),
@@ -353,9 +364,10 @@
             vmem((K + 16, VOC), BF16),
             vmem((NY, K, TILE), F32),
             vmem((PEERS, OWN, 256), BF16),
-            vmem((PEERS, OWN, 256), BF16),
+            vmem((NY - 1, OWN, 256), BF16),
+            vmem((NY, NX, OWN, 256), BF16),
+            vmem((NY, OWN, 256), BF16),
             vmem((OWN, 128), F32),
-            vmem((EX, K * K), F32),
             vmem((PEERS, EX, BLK), BF16),
             vmem((2, PEERS, EX, BLK), BF16),
             vmem((PEERS, EX, BLK), BF16),
@@ -363,19 +375,20 @@
             vmem((PEERS, ROWS, BLK), BF16),
             vmem((2, BLK, 128), F32),
             vmem((BLK, 128), F32),
-            vmem((BLK, 128), F32),
             dma((4 + NY,)),
-            dma, dma,
+            dma, dma((NY,)), dma,
             dma((3,)), dma((3,)),
             dma((2,)), dma((16,)), dma((15,)),
             dma, dma,
-            dma((2,)),
         ],
         compiler_params=pltpu.CompilerParams(
-            collective_id=0, has_side_effects=True, vmem_limit_bytes=58 * 1024 * 1024
+            collective_id=0, has_side_effects=True, vmem_limit_bytes=40 * 1024 * 1024
         ),
         cost_estimate=pl.CostEstimate(flops=500_000_000, bytes_accessed=4_000_000, transcendentals=1_100_000),
-    )(logits.T, labels.reshape(NY, TILE), activations.T, proj_in.T, proj_out.T)
+    )(*(
+        pltpu.with_memory_space_constraint(a, pltpu.HBM)
+        for a in (logits.T, labels.reshape(NY, TILE), activations.T, proj_in.T, proj_out.T)
+    ))
 
 
 def solution(mesh):

time: 49.9 us -> 46.9 us (0.940)
  local copies, waits for them, and re-layouts: 3.04 us -> 1.29 us
  Pallas kernels: 46 us -> 44.8 us
    unnamed x2, local copies, waits for them, and re-layouts: 3.04 us -> 1.29 us
    pallas_call x1, Pallas kernels: 46 us -> 44.8 us  [body(): pl.pallas_call(kernel, out_shape=(jax.ShapeDtypeStruct((EX, K * K), F32),...]
where the time goes in v4:
time: 46.9 us; the launch traced here: 46.7 us
  Pallas kernels  44.8 us (96%)
  local copies, waits for them, and re-layouts  1.29 us (3%)
  between operations  0.64 us (1%)
    pallas_call x1, Pallas kernels, body(): pl.pallas_call(kernel, out_shape=(jax.ShapeDtypeStruct((EX, K * K), F32),...  44.8 us
    unnamed x2, local copies, waits for them, and re-layouts  1.29 us

profile of v4, /device:TPU:1, one launch (start us, length us, event | category | flops | bytes accessed | tf_op | source)
XLA Modules:
  0.0 46.7 jit_solution(2603730777006834129)
XLA Ops:
  0.6 44.8 %shard_map.68 = (f32[4,4096]{1,0:T(4,128)S(1)}, f32[256,128]{1,0:T(8,128)S(1)}) custom-call(bf16[2000,512]{1,0:T(8,128)(2,1)} %bitcast.5, s32[4,128]{1,0:T(4,128)} %bitcast.9, bf16[320,512]{1,0:T(8,128)(2,1)} %bitcast.6, bf16[64,320]{1,0:T(8,128)(2,1)} %bitcast.8, bf16[64,2000]{1,0:T(8,128)(2,1)} %bitcast.7), custom_call_target="tpu_custom_call" | custom-call | flops 500000000 | bytes 4000000 | tf_op jit(solution)/shard_map/pallas_call | solution.py:351
  45.4 0.6 %copy.9 = f32[4,4096]{1,0:T(4,128)} copy(f32[4,4096]{1,0:T(4,128)S(1)} %get-tuple-element.4) | data formatting | bytes 131072
  46.1 0.7 %copy.10 = f32[256,128]{1,0:T(8,128)} copy(f32[256,128]{1,0:T(8,128)S(1)} %get-tuple-element.5) | data formatting | bytes 262144

commit v5 on v4

--- a/solution.py
+++ b/solution.py
@@ -190,8 +190,8 @@
         for both, wide in halves:
             first, second = both[:, K + 2 * k : K + 2 * k + 1], both[:, K + 2 * k + 1 : K + 2 * k + 2]
             value += jnp.where(lane < K, first, second) * wide
+        feat[:, k * 128 : (k + 1) * 128] = value
         value = value[0:EX] + value[EX:8]
-        feat[:, k * 128 : (k + 1) * 128] = value
         pieces[k // 2, :, (k % 2) * 128 : (k % 2 + 1) * 128] = value.astype(BF16)
 
     def send_row(group, block, far):
@@ -200,10 +200,6 @@
             recv_sem=a2a_recv.at[2 * far], device_id=dev(group, block), device_id_type=MESH,
         ).start()
 
-    for k in range(1, PEERS):
-        send_row(c, lax.rem(f + k, PEERS), 0)
-    for k in range(PEERS):
-        send_row(y_far, lax.rem(f + k, PEERS), 1)
 
     def send_col(block):
         pltpu.make_async_remote_copy(
@@ -222,6 +218,10 @@
     def _():
         col_in[f] = pieces[c]
 
+    for k in range(1, PEERS):
+        send_row(c, lax.rem(f + k, PEERS), 0)
+    for k in range(PEERS):
+        send_row(y_far, lax.rem(f + k, PEERS), 1)
     row_in[0, f] = pieces[f]
     wait_bytes(psend.at[pl.ds(0, PEERS - 1)], rs_send)
 
@@ -339,20 +339,21 @@
         device_id=partner, device_id_type=MESH,
     )
     swap.start()
+    gout[0] = acc[core]
     wait_bytes(rows.at[pl.ds(0, NZ - 1)], ag_send.at[0])
     wait_bytes(cols.at[pl.ds(0, PEERS - 1)], ag_send.at[1])
     swap.wait_recv()
-    gout[...] = acc[core] + xrecv[...]
+    gout[1] = xrecv[...]
     swap.wait_send()
 
 
 def body(logits, labels, activations, proj_in, proj_out):
     dma, vmem = pltpu.SemaphoreType.DMA, pltpu.VMEM
-    return pl.pallas_call(
+    feat, gram = pl.pallas_call(
         kernel,
         out_shape=(
-            jax.ShapeDtypeStruct((EX, K * K), F32),
-            jax.ShapeDtypeStruct((BLK, BLK // 2), F32),
+            jax.ShapeDtypeStruct((2 * EX, K * K), F32),
+            jax.ShapeDtypeStruct((2, BLK, BLK // 2), F32),
         ),
         in_specs=[pl.BlockSpec(memory_space=pltpu.HBM)] * 5,
         out_specs=(pl.BlockSpec(memory_space=pltpu.VMEM),) * 2,
@@ -389,6 +390,7 @@
         pltpu.with_memory_space_constraint(a, pltpu.HBM)
         for a in (logits.T, labels.reshape(NY, TILE), activations.T, proj_in.T, proj_out.T)
     ))
+    return feat[:EX] + feat[EX:], gram[0] + gram[1]
 
 
 def solution(mesh):

time: 46.9 us -> 46.7 us (level)
  other arithmetic: 0 us -> 1.32 us
  local copies, waits for them, and re-layouts: 1.29 us -> 0 us
    add x0 -> x2, other arithmetic: none -> 1.32 us  [body(): return (feat[:EX] + feat[EX:], gram[0] + gram[1])]
    unnamed x2 -> x0, local copies, waits for them, and re-layouts: 1.29 us -> none
where the time goes in v5:
time: 46.7 us; the launch traced here: 46.5 us
  Pallas kernels  44.6 us (96%)
  other arithmetic  1.32 us (3%)
  between operations  0.64 us (1%)
    pallas_call x1, Pallas kernels, body(): pl.pallas_call(kernel, out_shape=(jax.ShapeDtypeStruct((2 * EX, K * K), F...  44.6 us
    add x2, other arithmetic, body(): return (feat[:EX] + feat[EX:], gram[0] + gram[1])  1.32 us

profile of v5, /device:TPU:1, one launch (start us, length us, event | category | flops | bytes accessed | tf_op | source)
XLA Modules:
  0.0 46.5 jit_solution(9031881658655586716)
XLA Ops:
  0.6 44.6 %shard_map.68 = (f32[8,4096]{1,0:T(8,128)S(1)}, f32[2,256,128]{2,1,0:T(8,128)S(1)}) custom-call(bf16[2000,512]{1,0:T(8,128)(2,1)} %bitcast.7, s32[4,128]{1,0:T(4,128)} %bitcast.11, bf16[320,512]{1,0:T(8,128)(2,1)} %bitcast.8, bf16[64,320]{1,0:T(8,128)(2,1)} %bitcast.10, bf16[64,2000]{1,0:T(8,128)(2,1)} %bitcast.9), custom_call_target="tpu_custom_call" | custom-call | flops 500000000 | bytes 4000000 | tf_op jit(solution)/shard_map/pallas_call | solution.py:352
  45.2 0.6 %slice_add_fusion = f32[4,4096]{1,0:T(4,128)} fusion(f32[8,4096]{1,0:T(8,128)S(1)} %get-tuple-element.4), kind=kLoop, calls=%fused_computation.1 | loop fusion | flops 16384 | bytes 196608 | tf_op jit(solution)/shard_map/add | solution.py:393
  45.8 0.7 %add_bitcast_fusion = f32[256,128]{1,0:T(8,128)} fusion(f32[2,256,128]{2,1,0:T(8,128)S(1)} %get-tuple-element.5), kind=kLoop, calls=%fused_computation | loop fusion | flops 32768 | bytes 393216 | tf_op jit(solution)/shard_map/add | solution.py:393
